TPU v7x, 256 devices: a whole 4x4x8 slice. The times are simulated.
256 devices in a mesh: gx: 32 (over y, z_lo, core), gy: 8 (over z_hi, x).
Axes of the slice: x: 4, y: 4, z: 8 (z_hi: 2, z_lo: 4; z = z_hi * 4 + z_lo), core: 2. Of those that a mesh axis runs over, the one named last changes fastest.
Arguments:
- control: bfloat16 [2048, 8, 2048], P('gx', None, 'gy'), may hold values from -6 to 6
- innovation: float32 [2048, 8, 2048], P('gx', None, 'gy'), may hold values from -6 to 6
- obs_weight: float32 [2048, 8, 2048], P('gx', None, 'gy'), may hold values from 0.5 to 4
- courant_x: float32 [2048, 8, 2048], P('gx', None, 'gy'), may hold values from -0.9 to 0.9
- courant_y: float32 [2048, 8, 2048], P('gx', None, 'gy'), may hold values from -0.9 to 0.9
- filter_x: bfloat16 [2048, 2048], P('gx'), may hold values from -3 to 3
- filter_y: bfloat16 [2048, 2048], P('gy'), may hold values from -3 to 3
Outputs:
- end_state: float32 [2048, 8, 2048], P('gx', None, 'gy')
- gradient: float32 [2048, 8, 2048], P('gx', None, 'gy')
All inputs are finite; a program needn't handle non-finite values.
Results may differ from a plain program's by a relative error of at most 0.0029.
Values may be sent and summed in bfloat16 or wider, within the bound.
A program may use at most 128 MiB of HBM per device.

v0:
```python
import jax
import jax.numpy as jnp
from jax import lax
from jax.sharding import PartitionSpec as P


def extended(array, sides, width):
    for axis, dim in sides:
        size, length = (lax.axis_size(axis), array.shape[dim])
        up = [(i, (i + 1) % size) for i in range(size - 1)]
        down = [(j, i) for i, j in up]
        last = lax.slice_in_dim(array, length - width, length, axis=dim)
        initial = lax.slice_in_dim(array, 0, width, axis=dim)
        before = lax.ppermute(last, axis, up)
        after = lax.ppermute(initial, axis, down)
        array = jnp.concatenate([before, array, after], axis=dim)
    return array


def per_device(control, innovation, obs_weight, courant_x, courant_y, filter_x, filter_y):
    columns = filter_x
    smoothed = jnp.einsum(
        "ij,jlc->ilc",
        columns,
        lax.all_gather(control, "gx", axis=0, tiled=True),
        preferred_element_type=jnp.float32,
    ).astype(jnp.bfloat16)
    columns = filter_y
    start_state = jnp.einsum(
        "kc,xlc->xlk",
        columns,
        lax.all_gather(smoothed, "gy", axis=2, tiled=True),
        preferred_element_type=jnp.float32,
    )
    padded = extended(start_state, (("gx", 0), ("gy", 2)), 1)
    end_state = (
        start_state
        - courant_x * (padded[2:, :, 1:-1] - padded[:-2, :, 1:-1]) * 0.5
        - courant_y * (padded[1:-1, :, 2:] - padded[1:-1, :, :-2]) * 0.5
    )
    misfit = obs_weight * (end_state - innovation)
    fluxes = jnp.stack([courant_x * misfit, courant_y * misfit])
    rim_cells = extended(fluxes, (("gx", 1), ("gy", 3)), 1)
    adjoint = (
        misfit
        + 0.5 * (rim_cells[0, 2:, :, 1:-1] - rim_cells[0, :-2, :, 1:-1])
        + 0.5 * (rim_cells[1, 1:-1, :, 2:] - rim_cells[1, 1:-1, :, :-2])
    ).astype(jnp.bfloat16)
    partial_sums = jnp.einsum("kc,xlk->xlc", filter_y, adjoint, preferred_element_type=jnp.float32)
    pulled = lax.psum_scatter(partial_sums, "gy", scatter_dimension=2, tiled=True).astype(
        jnp.bfloat16
    )
    columns = filter_x
    carried = lax.psum_scatter(
        jnp.einsum("ij,ilc->jlc", columns, pulled, preferred_element_type=jnp.float32),
        "gx",
        scatter_dimension=0,
        tiled=True,
    )
    gradient = control.astype(jnp.float32) + carried
    return (end_state, gradient)


def solution(mesh):
    placed = (
        P("gx", None, "gy"),
        P("gx", None, "gy"),
        P("gx", None, "gy"),
        P("gx", None, "gy"),
        P("gx", None, "gy"),
        P("gx", None),
        P("gy", None),
    )
    return jax.shard_map(
        per_device,
        mesh=mesh,
        in_specs=placed,
        out_specs=(P("gx", None, "gy"), P("gx", None, "gy")),
        check_vma=False,
    )
```

profile of v0, /device:TPU:2, one launch (start us, length us, event | category | flops | bytes accessed | tf_op | source)
XLA Modules:
  0.0 578.3 jit_solution(11222078684383102453)
XLA Ops:
  7.2 0.7 all-gather.3.cloned.1.call-update
  8.0 74.1 %all-gather.3.cloned.1.call-done = bf16[2048,8,256]{2,1,0:T(8,128)(2,1)} async-done(((bf16[64,8,256]{2,1,0:T(8,128)(2,1)}), bf16[2048,8,256]{2,1,0:T(8,128)(2,1)}) %all-gather.3.cloned.1.call-update) | async-done | bytes 8388624 | tf_op jit(solution)/shard_map/all_gather | solution.py:25
  82.0 5.1 fusion
  87.1 0.9 copy.24
  88.1 75.3 %all-gather.5.cloned.1.call-done = bf16[64,8,2048]{2,1,0:T(8,128)(2,1)} async-done(((bf16[64,8,256]{2,1,0:T(8,128)(2,1)}), bf16[64,8,2048]{2,1,0:T(8,128)(2,1)}) %all-gather.5.cloned.1.call-update) | async-done | bytes 2097168 | tf_op jit(solution)/shard_map/all_gather | solution.py:32
  163.4 2.3 fusion.4
  165.7 1.3 collective-permute-start.1
  167.0 1.3 collective-permute-start
  168.4 2.7 collective-permute-done
  171.2 2.8 collective-permute-start.2
  174.0 3.1 collective-permute-start.3
  177.0 3.9 collective-permute-done.2
  180.9 3.1 collective-permute-done.3
  184.0 2.4 multiply_bitcast_fusion.1
  186.6 2.9 collective-permute-start.5
  189.5 1.3 collective-permute-start.4
  190.8 3.1 collective-permute-done.4
  193.9 1.0 fusion.28
  194.9 1.3 copy.11
  196.2 1.9 collective-permute-start.6
  198.1 0.3 copy.13
  198.4 3.9 collective-permute-start.7
  202.3 0.3 copy.12
  202.7 1.3 collective-permute-done.7
  203.9 1.1 copy.14
  205.0 1.4 fusion.10
  206.4 2.7 fusion.2
  209.1 145.5 %reduce-scatter.3.cloned.1.call-done = f32[64,8,256]{2,0,1:T(8,128)} async-done(((f32[64,8,2048]{2,0,1:T(8,128)}), f32[64,8,256]{2,0,1:T(8,128)}) %reduce-scatter.3.cloned.1.call-update) | async-done | bytes 524304 | tf_op jit(solution)/shard_map/reduce_scatter | solution.py:50
  354.6 9.1 %convolution_bitcast_fusion = f32[2048,8,256]{0,2,1:T(8,128)} fusion(bf16[64,2048]{1,0:T(8,128)(2,1)S(1)} %copy-done.4, f32[64,8,256]{2,0,1:T(8,128)} %reduce-scatter.3.cloned.1.call-done), kind=kOutput, calls=%fused_computation.2 | convolution fusion | flops 537001984 | bytes 17563648 | tf_op jit(solution)/shard_map/ij,ilc->jlc/dot_general | solution.py:55
  363.8 17.8 %copy.15 = f32[2048,8,256]{2,1,0:T(8,128)} copy(f32[2048,8,256]{0,2,1:T(8,128)} %convolution_bitcast_fusion) | data formatting | bytes 33554432 | tf_op jit(solution)/shard_map/ij,ilc->jlc/dot_general | solution.py:55
  381.6 188.3 %reduce-scatter.5.cloned.1.call-done = f32[64,8,256]{2,1,0:T(8,128)} async-done(((f32[2048,8,256]{2,1,0:T(8,128)}), f32[64,8,256]{2,1,0:T(8,128)}) %reduce-scatter.5.cloned.1.call-update) | async-done | bytes 524304 | tf_op jit(solution)/shard_map/reduce_scatter | solution.py:54
  569.9 1.9 convert_add_fusion
  (26 shorter events, 0.6 us)
Async XLA Ops:
  7.2 156.2 %copy-start = (bf16[256,2048]{1,0:T(8,128)(2,1)S(1)}, bf16[256,2048]{1,0:T(8,128)(2,1)}, u32[]{:S(2)}) copy-start(bf16[256,2048]{1,0:T(8,128)(2,1)} %param.13) | copy-start | bytes 3145732
  7.2 74.9 %all-gather.3.cloned.1.call-start = ((), (), s32[]{:S(2)}) async-start(), calls=%async_computation.2 | async-start | bytes 8650752 | tf_op jit(solution)/shard_map/all_gather | solution.py:25
  7.9 155.5 %all-gather.5.cloned.1.call-start = ((), (), s32[]{:S(2)}) async-start(), calls=%async_computation.3 | async-start | bytes 2359296 | tf_op jit(solution)/shard_map/all_gather | solution.py:32
  88.0 96.0 %copy-start.1 = (f32[64,8,256]{2,1,0:T(8,128)S(1)}, f32[64,8,256]{2,1,0:T(8,128)}, u32[]{:S(2)}) copy-start(f32[64,8,256]{2,1,0:T(8,128)} %param.11) | copy-start | bytes 1572868
  88.0 96.0 %copy-start.3 = (f32[64,8,256]{2,1,0:T(8,128)S(1)}, f32[64,8,256]{2,1,0:T(8,128)}, u32[]{:S(2)}) copy-start(f32[64,8,256]{2,1,0:T(8,128)} %param.10) | copy-start | bytes 1572868
  88.0 266.6 %reduce-scatter.3.cloned.1.call-start = ((), (), s32[]{:S(2)}) async-start(), calls=%async_computation.4 | async-start | bytes 4718592 | tf_op jit(solution)/shard_map/reduce_scatter | solution.py:50
  165.7 2.6 collective-permute-start.1
  167.0 4.0 collective-permute-start
  171.2 9.8 %collective-permute-start.2 = (f32[66,8,1]{2,1,0:T(8,128)S(1)}, f32[66,8,1]{2,1,0:T(8,128)S(1)}, u32[]{:S(2)}, u32[]{:S(2)}) collective-permute-start(f32[66,8,1]{2,1,0:T(8,128)S(1)} %get-tuple-element.11), channel_id=1, source_target_pairs={{1,0},{2,1},{3,2},{4,3},{5,4},{6,5},{7,6},{9,8},{10,9},{11,10},{12... | collective-permute-start | bytes 6344 | tf_op jit(solution)/shard_map/ppermute | solution.py:15
  174.0 10.1 %collective-permute-start.3 = (f32[66,8,1]{2,1,0:T(8,128)S(1)}, f32[66,8,1]{2,1,0:T(8,128)S(1)}, u32[]{:S(2)}, u32[]{:S(2)}) collective-permute-start(f32[66,8,1]{2,1,0:T(8,128)S(1)} %get-tuple-element.12), channel_id=1, source_target_pairs={{0,1},{1,2},{2,3},{3,4},{4,5},{5,6},{6,7},{8,9},{9,10},{10,11},{11... | collective-permute-start | bytes 6344 | tf_op jit(solution)/shard_map/ppermute | solution.py:14
  186.6 4.2 collective-permute-start.5
  189.5 4.4 collective-permute-start.4
  196.2 6.1 %collective-permute-start.6 = (f32[2,66,8,1]{1,2,3,0:T(8,128)S(1)}, f32[2,66,8,1]{1,2,3,0:T(8,128)S(1)}, u32[]{:S(2)}, u32[]{:S(2)}) collective-permute-start(f32[2,66,8,1]{1,2,3,0:T(8,128)S(1)} %copy.11), channel_id=1, source_target_pairs={{1,0},{2,1},{3,2},{4,3},{5,4},{6,5},{7,6},{9,8},{10,9},{11,10},{12... | collective-permute-start | bytes 12680 | tf_op jit(solution)/shard_map/ppermute | solution.py:15
  198.4 5.5 collective-permute-start.7
  209.1 145.6 %copy-start.4 = (bf16[64,2048]{1,0:T(8,128)(2,1)S(1)}, bf16[64,2048]{1,0:T(8,128)(2,1)}, u32[]{:S(2)}) copy-start(bf16[64,2048]{1,0:T(8,128)(2,1)} %param.12) | copy-start | bytes 786436
  209.1 360.8 %reduce-scatter.5.cloned.1.call-start = ((), (), s32[]{:S(2)}) async-start(), calls=%async_computation.5 | async-start | bytes 17301504 | tf_op jit(solution)/shard_map/reduce_scatter | solution.py:54
  381.6 188.3 %copy-start.2 = (bf16[64,8,256]{2,1,0:T(8,128)(2,1)S(1)}, bf16[64,8,256]{2,1,0:T(8,128)(2,1)}, u32[]{:S(2)}) copy-start(bf16[64,8,256]{2,1,0:T(8,128)(2,1)} %param.7) | copy-start | bytes 786436
Sparse Core Ops, SparseCore 0:
  9.9 72.1 all-gather.2
  88.1 75.2 all-gather.4
  209.2 145.3 reduce-scatter.2
  381.7 188.1 reduce-scatter.4
where the time goes:
time: 579 us; the launch traced here: 578 us
  waiting for transfers between devices  498 us (86%)
  local copies, waits for them, and re-layouts  22.8 us (4%)
  matrix products  19.2 us (3%)
  starting transfers between devices  18.6 us (3%)
  between operations  13.9 us (2%)
  other arithmetic  5.88 us (1%)
    reduce_scatter x1, waiting for transfers between devices, per_device(): lax.psum_scatter(jnp.einsum('ij,ilc->jlc', columns, pulled, preferred_ele...  188 us
    reduce_scatter x1, waiting for transfers between devices, per_device(): lax.psum_scatter(partial_sums, 'gy', scatter_dimension=2, tiled=True)  145 us
    all_gather x1, waiting for transfers between devices, per_device(): lax.all_gather(smoothed, 'gy', axis=2, tiled=True)  75.3 us
    all_gather x1, waiting for transfers between devices, per_device(): lax.all_gather(control, 'gx', axis=0, tiled=True)  74.1 us
    dot_general x1, local copies, waits for them, and re-layouts, per_device(): jnp.einsum('ij,ilc->jlc', columns, pulled, preferred_element_type=jnp.flo...  17.8 us
  transfers between devices with their start and end apart: 12, of which 9 were waited for; matrix products, arithmetic and copies ran while one was open for 0% of the time, Pallas kernels for 0%

commit v1 on v0

--- a/solution.py
+++ b/solution.py
@@ -29,7 +29,9 @@
     start_state = jnp.einsum(
         "kc,xlc->xlk",
         columns,
-        lax.all_gather(smoothed, "gy", axis=2, tiled=True),
+        jnp.concatenate(
+            lax.all_to_all(jnp.stack([smoothed] * lax.axis_size("gy")), "gy", 0, 0), axis=2
+        ),
         preferred_element_type=jnp.float32,
     )
     padded = extended(start_state, (("gx", 0), ("gy", 2)), 1)

time: 579 us -> 559 us (0.965)
  waiting for transfers between devices: 498 us -> 421 us
  blocking collectives: 0 us -> 58.3 us
    all_gather x1 -> x0, waiting for transfers between devices: 75.3 us -> none  [per_device(): lax.all_gather(smoothed, 'gy', axis=2, tiled=True)]
    all_to_all x0 -> x1, blocking collectives: none -> 58.3 us  [per_device(): lax.all_to_all(jnp.stack([smoothed] * lax.axis_size('gy')), 'gy', 0, 0)]
  transfers between devices with their start and end apart: 12 -> 11, of which waited for: 9 -> 8; matrix products, arithmetic and copies ran while one was open for 0% -> 0% of each run, Pallas kernels for 0% -> 0%
where the time goes in v1:
time: 559 us
  waiting for transfers between devices  421 us (75%)
  blocking collectives  58.3 us (10%)
  local copies, waits for them, and re-layouts  24.3 us (4%)
  starting transfers between devices  18.6 us (3%)
  matrix products  17.6 us (3%)
  between operations  14 us (3%)
    reduce_scatter x1, waiting for transfers between devices, per_device(): lax.psum_scatter(jnp.einsum('ij,ilc->jlc', columns, pulled, preferred_ele...  188 us
    reduce_scatter x1, waiting for transfers between devices, per_device(): lax.psum_scatter(partial_sums, 'gy', scatter_dimension=2, tiled=True)  142 us
    all_gather x1, waiting for transfers between devices, per_device(): lax.all_gather(control, 'gx', axis=0, tiled=True)  73.7 us
    all_to_all x1, blocking collectives, per_device(): lax.all_to_all(jnp.stack([smoothed] * lax.axis_size('gy')), 'gy', 0, 0)  58.3 us
    dot_general x1, local copies, waits for them, and re-layouts, per_device(): jnp.einsum('ij,ilc->jlc', columns, pulled, preferred_element_type=jnp.flo...  17.8 us
    ppermute x4, waiting for transfers between devices, extended(): after = lax.ppermute(initial, axis, down)  12.2 us
  transfers between devices with their start and end apart: 11, of which 8 were waited for; matrix products, arithmetic and copies ran while one was open for 0% of the time, Pallas kernels for 0%

profile of v1, /device:TPU:2, one launch (start us, length us, event | category | flops | bytes accessed | tf_op | source)
XLA Modules:
  0.0 558.7 jit_solution(6831188639178378537)
XLA Ops:
  7.2 1.8 copy.13
  9.1 73.7 %all-gather.2.cloned.1.call-done = bf16[2048,8,256]{2,0,1:T(8,128)(2,1)} async-done(((bf16[64,8,256]{2,0,1:T(8,128)(2,1)}), bf16[2048,8,256]{2,0,1:T(8,128)(2,1)}) %all-gather.2.cloned.1.call-update) | async-done | bytes 8388624 | tf_op jit(solution)/shard_map/all_gather | solution.py:25
  82.8 5.0 convolution_convert_fusion
  88.1 58.3 %all_to_all.5 = bf16[8,64,8,256]{3,2,1,0:T(8,128)(2,1)S(1)} all-to-all(bf16[8,64,8,256]{3,2,1,0:T(8,128)(2,1)S(1)} %stack.8), channel_id=1, replica_groups=mesh['gx'=32,'gy'=8] {'gy'}, dimensions={0} | all-to-all | bytes 4194304 | tf_op jit(solution)/shard_map/all_to_all | solution.py:33
  146.5 0.3 copy.15
  146.8 0.8 fusion.2
  147.6 1.3 collective-permute-start.1
  148.9 1.3 collective-permute-start
  150.2 4.8 collective-permute-done
  155.2 3.6 collective-permute-start.2
  158.8 2.2 collective-permute-start.3
  161.0 3.9 collective-permute-done.2
  164.9 4.0 collective-permute-done.3
  168.9 1.2 multiply_bitcast_fusion.1
  170.2 2.9 collective-permute-start.5
  173.1 1.3 collective-permute-start.4
  174.4 3.5 collective-permute-done.4
  178.1 1.0 fusion.26
  179.0 1.3 copy.16
  180.3 1.9 collective-permute-start.6
  182.3 0.3 copy.18
  182.5 3.9 collective-permute-start.7
  186.5 0.3 copy.17
  186.8 1.3 collective-permute-done.7
  188.1 1.1 copy.19
  189.2 1.4 fusion.8
  190.5 2.6 fusion
  193.3 141.8 %reduce-scatter.3.cloned.1.call-done = f32[64,8,256]{2,0,1:T(8,128)} async-done(((f32[64,8,2048]{2,0,1:T(8,128)}), f32[64,8,256]{2,0,1:T(8,128)}) %reduce-scatter.3.cloned.1.call-update) | async-done | bytes 524304 | tf_op jit(solution)/shard_map/reduce_scatter | solution.py:52
  335.0 9.1 %convolution_bitcast_fusion = f32[2048,8,256]{0,2,1:T(8,128)} fusion(bf16[64,2048]{1,0:T(8,128)(2,1)S(1)} %copy-done.2, f32[64,8,256]{2,0,1:T(8,128)} %reduce-scatter.3.cloned.1.call-done), kind=kOutput, calls=%fused_computation | convolution fusion | flops 537001984 | bytes 17563648 | tf_op jit(solution)/shard_map/ij,ilc->jlc/dot_general | solution.py:57
  344.2 17.8 %copy.20 = f32[2048,8,256]{2,1,0:T(8,128)} copy(f32[2048,8,256]{0,2,1:T(8,128)} %convolution_bitcast_fusion) | data formatting | bytes 33554432 | tf_op jit(solution)/shard_map/ij,ilc->jlc/dot_general | solution.py:57
  362.0 188.3 %reduce-scatter.5.cloned.1.call-done = f32[64,8,256]{2,1,0:T(8,128)} async-done(((f32[2048,8,256]{2,1,0:T(8,128)}), f32[64,8,256]{2,1,0:T(8,128)}) %reduce-scatter.5.cloned.1.call-update) | async-done | bytes 524304 | tf_op jit(solution)/shard_map/reduce_scatter | solution.py:56
  550.3 1.9 convert_add_fusion
  (31 shorter events, 0.8 us)
Async XLA Ops:
  7.2 139.6 %copy-start = (bf16[256,2048]{1,0:T(8,128)(2,1)S(1)}, bf16[256,2048]{1,0:T(8,128)(2,1)}, u32[]{:S(2)}) copy-start(bf16[256,2048]{1,0:T(8,128)(2,1)} %param.13) | copy-start | bytes 3145732
  7.2 75.6 %all-gather.2.cloned.1.call-start = ((), (), s32[]{:S(2)}) async-start(), calls=%async_computation.3 | async-start | bytes 8650752 | tf_op jit(solution)/shard_map/all_gather | solution.py:25
  9.0 326.0 %reduce-scatter.3.cloned.1.call-start = ((), (), s32[]{:S(2)}) async-start(), calls=%async_computation.4 | async-start | bytes 4718592 | tf_op jit(solution)/shard_map/reduce_scatter | solution.py:52
  146.7 22.2 %copy-start.1 = (f32[64,8,256]{2,1,0:T(8,128)S(1)}, f32[64,8,256]{2,1,0:T(8,128)}, u32[]{:S(2)}) copy-start(f32[64,8,256]{2,1,0:T(8,128)} %param.11) | copy-start | bytes 1572868
  146.8 22.1 %copy-start.4 = (f32[64,8,256]{2,1,0:T(8,128)S(1)}, f32[64,8,256]{2,1,0:T(8,128)}, u32[]{:S(2)}) copy-start(f32[64,8,256]{2,1,0:T(8,128)} %param.10) | copy-start | bytes 1572868
  146.8 22.1 %copy-start.5 = (f32[64,8,256]{2,1,0:T(8,128)S(1)}, f32[64,8,256]{2,1,0:T(8,128)}, u32[]{:S(2)}) copy-start(f32[64,8,256]{2,1,0:T(8,128)} %param.9) | copy-start | bytes 1572868
  146.8 22.1 %copy-start.6 = (f32[64,8,256]{2,1,0:T(8,128)S(1)}, f32[64,8,256]{2,1,0:T(8,128)}, u32[]{:S(2)}) copy-start(f32[64,8,256]{2,1,0:T(8,128)} %param.8) | copy-start | bytes 1572868
  147.6 2.6 collective-permute-start.1
  148.9 6.1 %collective-permute-start = (f32[1,8,256]{2,1,0:T(8,128)S(1)}, f32[1,8,256]{2,1,0:T(8,128)S(1)}, u32[]{:S(2)}, u32[]{:S(2)}) collective-permute-start(f32[1,8,256]{2,1,0:T(8,128)S(1)} %get-tuple-element.14), channel_id=1, source_target_pairs={{8,0},{16,8},{24,16},{32,24},{40,32},{48,40},{56,48},{64,56},{72,6... | collective-permute-start | bytes 24584 | tf_op jit(solution)/shard_map/ppermute | solution.py:15
  155.2 9.8 %collective-permute-start.2 = (f32[66,8,1]{2,1,0:T(8,128)S(1)}, f32[66,8,1]{2,1,0:T(8,128)S(1)}, u32[]{:S(2)}, u32[]{:S(2)}) collective-permute-start(f32[66,8,1]{2,1,0:T(8,128)S(1)} %get-tuple-element.11), channel_id=1, source_target_pairs={{1,0},{2,1},{3,2},{4,3},{5,4},{6,5},{7,6},{9,8},{10,9},{11,10},{12... | collective-permute-start | bytes 6344 | tf_op jit(solution)/shard_map/ppermute | solution.py:15
  158.8 10.1 %collective-permute-start.3 = (f32[66,8,1]{2,1,0:T(8,128)S(1)}, f32[66,8,1]{2,1,0:T(8,128)S(1)}, u32[]{:S(2)}, u32[]{:S(2)}) collective-permute-start(f32[66,8,1]{2,1,0:T(8,128)S(1)} %get-tuple-element.12), channel_id=1, source_target_pairs={{0,1},{1,2},{2,3},{3,4},{4,5},{5,6},{6,7},{8,9},{9,10},{10,11},{11... | collective-permute-start | bytes 6344 | tf_op jit(solution)/shard_map/ppermute | solution.py:14
  170.2 4.2 collective-permute-start.5
  173.1 4.9 collective-permute-start.4
  180.3 6.1 %collective-permute-start.6 = (f32[2,66,8,1]{1,2,3,0:T(8,128)S(1)}, f32[2,66,8,1]{1,2,3,0:T(8,128)S(1)}, u32[]{:S(2)}, u32[]{:S(2)}) collective-permute-start(f32[2,66,8,1]{1,2,3,0:T(8,128)S(1)} %copy.16), channel_id=1, source_target_pairs={{1,0},{2,1},{3,2},{4,3},{5,4},{6,5},{7,6},{9,8},{10,9},{11,10},{12... | collective-permute-start | bytes 12680 | tf_op jit(solution)/shard_map/ppermute | solution.py:15
  182.5 5.5 collective-permute-start.7
  193.2 141.8 %copy-start.2 = (bf16[64,2048]{1,0:T(8,128)(2,1)S(1)}, bf16[64,2048]{1,0:T(8,128)(2,1)}, u32[]{:S(2)}) copy-start(bf16[64,2048]{1,0:T(8,128)(2,1)} %param.12) | copy-start | bytes 786436
  193.2 357.1 %reduce-scatter.5.cloned.1.call-start = ((), (), s32[]{:S(2)}) async-start(), calls=%async_computation.5 | async-start | bytes 17301504 | tf_op jit(solution)/shard_map/reduce_scatter | solution.py:56
  362.0 188.3 %copy-start.3 = (bf16[64,8,256]{2,1,0:T(8,128)(2,1)S(1)}, bf16[64,8,256]{2,1,0:T(8,128)(2,1)}, u32[]{:S(2)}) copy-start(bf16[64,8,256]{2,1,0:T(8,128)(2,1)} %param.7) | copy-start | bytes 786436
Sparse Core Ops, SparseCore 0:
  10.5 72.3 all-gather.1
  193.3 141.6 reduce-scatter.2
  362.1 188.1 reduce-scatter.4
